TPU v7x, 32 devices: a whole 2x2x4 slice. The times are simulated.
32 devices in a mesh: gx: 4 (over y, x), gy: 8 (over z, core).
Axes of the slice: x: 2, y: 2, z: 4, core: 2. Of those that a mesh axis runs over, the one named last changes fastest.
Arguments:
- forcing: float32 [4, 2, 256, 1024], P(None, None, 'gx', 'gy'), may hold values from -18 to 18
- observed: float32 [4, 2, 256, 1024], P(None, None, 'gx', 'gy'), may hold values from -6 to 6
- viscosity: float32 [256, 1024], P('gx', 'gy'), may hold values from 0.05 to 0.5
- friction: float32 [256, 1024], P('gx', 'gy'), may hold values from 0.2 to 2
- ice_mask: int32 [256, 1024], P('gx', 'gy'), may hold values from 0 to 2
- dirichlet: int32 [256, 1024], P('gx', 'gy'), may hold values 0 or 1
Outputs:
- velocity: float32 [4, 2, 256, 1024], P(None, None, 'gx', 'gy')
- gradient: float32 [256, 1024], P('gx', 'gy')
All inputs are finite; a program needn't handle non-finite values. No bound on the sum of `dirichlet` on one device may be relied on, other than what follows from the above.
Results may differ from a plain program's by a relative error of at most 0.00002.
Values sent between devices are 32-bit elements; how exact they have to be, the bound alone decides.
A program may use at most 64 MiB of HBM per device.

v0:
```python
import jax
import jax.numpy as jnp
from jax import lax
from jax.sharding import PartitionSpec as P

SWEEPS = 3


UPPER_BOUND = 2.4
LOWER_BOUND = 0.05
FREE_DRAG = 4.0


def extended_2(shard, sides, width):
    for axis, dim in sides:
        size, length = (lax.axis_size(axis), shard.shape[dim])
        up = [(i, (i + 1) % size) for i in range(size - 1)]
        down = [(j, i) for i, j in up]
        last = lax.slice_in_dim(shard, length - width, length, axis=dim)
        initial = lax.slice_in_dim(shard, 0, width, axis=dim)
        before = lax.ppermute(last, axis, up)
        after = lax.ppermute(initial, axis, down)
        shard = jnp.concatenate([before, shard, after], axis=dim)
    return shard


def shifted(block, axis, distance):
    devices = range(lax.axis_size(axis))
    route = [(i - distance, i) for i in devices if i - distance in devices]
    return lax.ppermute(block, axis, route)


def face_values(eta_ext):
    centre = eta_ext[1:-1, 1:-1]
    north = eta_ext[2:, 1:-1]
    south = eta_ext[:-2, 1:-1]
    east = eta_ext[1:-1, 2:]
    west = eta_ext[1:-1, :-2]
    return (
        north,
        south,
        east,
        west,
        0.5 * (centre + north),
        0.5 * (centre + south),
        0.5 * (centre + east),
        0.5 * (centre + west),
    )


def stencil_apply(field, eta_ext, node_drag):
    north, south, east, west, face_np, face_sm, face_ep, face_wm = face_values(eta_ext)
    along_u = field[:, 0]
    along_v = field[:, 1]

    def normal_part(values, weight_rows, weight_cols):
        middle = values[:, 1:-1, 1:-1]
        rows_part = face_np * (values[:, 2:, 1:-1] - middle) - face_sm * (
            middle - values[:, :-2, 1:-1]
        )
        cols_part = face_ep * (values[:, 1:-1, 2:] - middle) - face_wm * (
            middle - values[:, 1:-1, :-2]
        )
        return weight_rows * rows_part + weight_cols * cols_part

    def cross_part(values, weight_rows, weight_cols):
        slope_cols = 0.5 * (values[:, :, 2:] - values[:, :, :-2])
        slope_rows = 0.5 * (values[:, 2:, :] - values[:, :-2, :])
        first = 0.5 * weight_rows * (north * slope_cols[:, 2:, :] - south * slope_cols[:, :-2, :])
        second = 0.5 * weight_cols * (east * slope_rows[:, :, 2:] - west * slope_rows[:, :, :-2])
        return first + second

    image_u = (
        node_drag * along_u[:, 1:-1, 1:-1]
        - normal_part(along_u, 4.0, 1.0)
        - cross_part(along_v, 2.0, 1.0)
    )
    image_v = (
        node_drag * along_v[:, 1:-1, 1:-1]
        - normal_part(along_v, 1.0, 4.0)
        - cross_part(along_u, 1.0, 2.0)
    )
    return jnp.stack([image_u, image_v], axis=1)


def diagonal_terms(eta_ext, node_drag):
    north, south, east, west, face_np, face_sm, face_ep, face_wm = face_values(eta_ext)
    rows_sum = face_np + face_sm
    cols_sum = face_ep + face_wm
    return jnp.stack(
        [4.0 * rows_sum + cols_sum + node_drag, rows_sum + 4.0 * cols_sum + node_drag], axis=0
    )


def trim_margin(field, width):
    rows = field.shape[-2]
    cols = field.shape[-1]
    return field[..., width : rows - width, width : cols - width]


def keep_field(field):
    return field


def chebyshev_local(rhs, current, margin, extend, grows, eta_big, node_drag, inverse_diag):
    centre_value = 0.5 * (UPPER_BOUND + LOWER_BOUND)
    half_width = 0.5 * (UPPER_BOUND - LOWER_BOUND)
    ratio_value = centre_value / half_width
    weight_now = 1.0 / ratio_value
    residual = rhs
    direction = trim_margin(inverse_diag, margin - current) * residual / centre_value
    iterate = jnp.zeros_like(rhs)
    for sweep_no in range(SWEEPS + 1):
        iterate = iterate + direction
        if sweep_no < SWEEPS:
            extended = extend(direction)
            outer = current + grows
            image = stencil_apply(
                extended,
                trim_margin(eta_big, margin + 1 - outer),
                trim_margin(node_drag, margin + 1 - outer),
            )
            shrink = current - (outer - 1)
            iterate = trim_margin(iterate, shrink)
            direction = trim_margin(direction, shrink)
            residual = trim_margin(residual, shrink) - image
            current = outer - 1
            weight_next = 1.0 / (2.0 * ratio_value - weight_now)
            scaled = trim_margin(inverse_diag, margin - current) * residual
            direction = (
                weight_next * weight_now * direction + 2.0 * weight_next / half_width * scaled
            )
            weight_now = weight_next
    return iterate


def body(forcing, observed, viscosity, friction, ice_mask, dirichlet):
    release = (1 - dirichlet).astype(jnp.float32)
    element_drag = jnp.where(ice_mask == 2, friction, jnp.where(ice_mask == 0, FREE_DRAG, 0.0))
    forward_rhs = release * forcing
    margin = SWEEPS
    stacked = extended_2(
        jnp.stack([viscosity, element_drag, release]), (("gx", 1), ("gy", 2)), SWEEPS + 1
    )
    release_big = trim_margin(stacked[2], 1)
    eta_big = stacked[0]
    drag_elems = stacked[1]
    node_drag = 0.25 * (
        drag_elems[:-2, :-2]
        + drag_elems[1:-1, :-2]
        + drag_elems[:-2, 1:-1]
        + drag_elems[1:-1, 1:-1]
    )
    inverse_diag = release_big / (diagonal_terms(eta_big, node_drag) + 1.0 - release_big)
    velocity = chebyshev_local(
        block_rhs_wide(forward_rhs), margin, margin, keep_field, 0, eta_big, node_drag, inverse_diag
    )
    misfit = release * (velocity - observed)
    adjoint = chebyshev_local(
        block_rhs_wide(misfit), margin, margin, keep_field, 0, eta_big, node_drag, inverse_diag
    )
    product = jnp.sum(adjoint * velocity, axis=(0, 1))
    next_row = shifted(product[0:1, :], "gx", -1)
    rows_ext = jnp.concatenate([product, next_row], axis=0)
    rows_sum = rows_ext[:-1] + rows_ext[1:]
    next_col = shifted(rows_sum[:, 0:1], "gy", -1)
    cols_ext = jnp.concatenate([rows_sum, next_col], axis=1)
    total = cols_ext[:, :-1] + cols_ext[:, 1:]
    grounded = (ice_mask == 2).astype(jnp.float32)
    gradient = -0.25 * grounded * total
    return (velocity, gradient)


def block_rhs_wide(field):
    return extended_2(field, (("gx", 2), ("gy", 3)), SWEEPS)


def solution(mesh):
    return jax.shard_map(
        body,
        mesh=mesh,
        in_specs=(
            P(None, None, "gx", "gy"),
            P(None, None, "gx", "gy"),
            P("gx", "gy"),
            P("gx", "gy"),
            P("gx", "gy"),
            P("gx", "gy"),
        ),
        out_specs=(P(None, None, "gx", "gy"), P("gx", "gy")),
        check_vma=False,
    )
```

profile of v0, /device:TPU:1, one launch (start us, length us, event | category | flops | bytes accessed | tf_op | source)
XLA Modules:
  0.0 115.6 jit_solution(2168023500601347567)
XLA Ops:
  0.6 0.8 copy.64
  1.5 0.7 copy-done.1
  2.3 0.7 copy-done.2
  3.1 0.7 copy-done.3
  4.0 4.0 %collective-permute-start = (f32[3,4,128]{1,2,0:T(8,128)S(1)}, f32[3,4,128]{1,2,0:T(8,128)S(1)}, u32[]{:S(2)}, u32[]{:S(2)}) collective-permute-start(f32[3,4,128]{1,2,0:T(8,128)S(1)} %get-tuple-element.50), channel_id=1, source_target_pairs={{0,8},{8,16},{16,24},{1,9},{9,17},{17,25},{2,10},{10,18},{18,26},{... | collective-permute-start | bytes 18440 | tf_op jit(solution)/shard_map/ppermute | solution.py:21
  8.0 1.3 %collective-permute-start.1 = (f32[3,4,128]{1,2,0:T(8,128)S(1)}, f32[3,4,128]{1,2,0:T(8,128)S(1)}, u32[]{:S(2)}, u32[]{:S(2)}) collective-permute-start(f32[3,4,128]{1,2,0:T(8,128)S(1)} %get-tuple-element.51), channel_id=1, source_target_pairs={{8,0},{16,8},{24,16},{9,1},{17,9},{25,17},{10,2},{18,10},{26,18},{... | collective-permute-start | bytes 18440 | tf_op jit(solution)/shard_map/ppermute | solution.py:22
  9.6 2.0 %collective-permute-done = f32[3,4,128]{1,2,0:T(8,128)S(1)} collective-permute-done((f32[3,4,128]{1,2,0:T(8,128)S(1)}, f32[3,4,128]{1,2,0:T(8,128)S(1)}, u32[]{:S(2)}, u32[]{:S(2)}) %collective-permute-start) | collective-permute-done | bytes 6176 | tf_op jit(solution)/shard_map/ppermute | solution.py:21
  11.5 6.2 %collective-permute-done.1 = f32[3,4,128]{1,2,0:T(8,128)S(1)} collective-permute-done((f32[3,4,128]{1,2,0:T(8,128)S(1)}, f32[3,4,128]{1,2,0:T(8,128)S(1)}, u32[]{:S(2)}, u32[]{:S(2)}) %collective-permute-start.1) | collective-permute-done | bytes 6176 | tf_op jit(solution)/shard_map/ppermute | solution.py:22
  17.8 4.6 %collective-permute-start.2 = (f32[3,72,4]{1,2,0:T(4,128)S(1)}, f32[3,72,4]{1,2,0:T(4,128)S(1)}, u32[]{:S(2)}, u32[]{:S(2)}) collective-permute-start(f32[3,72,4]{1,2,0:T(4,128)S(1)} %get-tuple-element.26), channel_id=1, source_target_pairs={{0,1},{1,2},{2,3},{3,4},{4,5},{5,6},{6,7},{8,9},{9,10},{10,11},{11... | collective-permute-start | bytes 10376 | tf_op jit(solution)/shard_map/ppermute | solution.py:21
  22.4 1.9 %collective-permute-start.3 = (f32[3,72,4]{1,2,0:T(4,128)S(1)}, f32[3,72,4]{1,2,0:T(4,128)S(1)}, u32[]{:S(2)}, u32[]{:S(2)}) collective-permute-start(f32[3,72,4]{1,2,0:T(4,128)S(1)} %get-tuple-element.27), channel_id=1, source_target_pairs={{1,0},{2,1},{3,2},{4,3},{5,4},{6,5},{7,6},{9,8},{10,9},{11,10},{12... | collective-permute-start | bytes 10376 | tf_op jit(solution)/shard_map/ppermute | solution.py:22
  24.3 1.0 fusion.228
  25.3 3.1 %collective-permute-start.4 = (f32[4,2,3,128]{2,3,0,1:T(8,128)}, f32[4,2,3,128]{2,3,0,1:T(8,128)S(1)}, u32[]{:S(2)}, u32[]{:S(2)}) collective-permute-start(f32[4,2,3,128]{2,3,0,1:T(8,128)} %get-tuple-element.45), channel_id=1, source_target_pairs={{0,8},{8,16},{16,24},{1,9},{9,17},{17,25},{2,10},{10,18},{18,26},{... | collective-permute-start | bytes 36872 | tf_op jit(solution)/shard_map/ppermute | solution.py:21
  28.5 1.3 %collective-permute-start.5 = (f32[4,2,3,128]{2,3,0,1:T(8,128)S(1)}, f32[4,2,3,128]{2,3,0,1:T(8,128)S(1)}, u32[]{:S(2)}, u32[]{:S(2)}) collective-permute-start(f32[4,2,3,128]{2,3,0,1:T(8,128)S(1)} %get-tuple-element.46), channel_id=1, source_target_pairs={{8,0},{16,8},{24,16},{9,1},{17,9},{25,17},{10,2},{18,10},{26,18},{... | collective-permute-start | bytes 36872 | tf_op jit(solution)/shard_map/ppermute | solution.py:22
  29.8 1.2 copy.66
  32.1 6.4 %collective-permute-done.4 = f32[4,2,3,128]{2,3,0,1:T(8,128)S(1)} collective-permute-done((f32[4,2,3,128]{2,3,0,1:T(8,128)}, f32[4,2,3,128]{2,3,0,1:T(8,128)S(1)}, u32[]{:S(2)}, u32[]{:S(2)}) %collective-permute-start.4) | collective-permute-done | bytes 12320 | tf_op jit(solution)/shard_map/ppermute | solution.py:21
  38.5 11.3 %collective-permute-done.5 = f32[4,2,3,128]{2,3,0,1:T(8,128)S(1)} collective-permute-done((f32[4,2,3,128]{2,3,0,1:T(8,128)S(1)}, f32[4,2,3,128]{2,3,0,1:T(8,128)S(1)}, u32[]{:S(2)}, u32[]{:S(2)}) %collective-permute-start.5) | collective-permute-done | bytes 12320 | tf_op jit(solution)/shard_map/ppermute | solution.py:22
  49.9 6.0 %collective-permute-start.6 = (f32[4,2,70,3]{2,3,0,1:T(4,128)S(1)}, f32[4,2,70,3]{2,3,0,1:T(4,128)S(1)}, u32[]{:S(2)}, u32[]{:S(2)}) collective-permute-start(f32[4,2,70,3]{2,3,0,1:T(4,128)S(1)} %get-tuple-element.24), channel_id=1, source_target_pairs={{0,1},{1,2},{2,3},{3,4},{4,5},{5,6},{6,7},{8,9},{9,10},{10,11},{11... | collective-permute-start | bytes 20168 | tf_op jit(solution)/shard_map/ppermute | solution.py:21
  56.0 1.9 %collective-permute-start.7 = (f32[4,2,70,3]{2,3,0,1:T(4,128)S(1)}, f32[4,2,70,3]{2,3,0,1:T(4,128)S(1)}, u32[]{:S(2)}, u32[]{:S(2)}) collective-permute-start(f32[4,2,70,3]{2,3,0,1:T(4,128)S(1)} %get-tuple-element.25), channel_id=1, source_target_pairs={{1,0},{2,1},{3,2},{4,3},{5,4},{6,5},{7,6},{9,8},{10,9},{11,10},{12... | collective-permute-start | bytes 20168 | tf_op jit(solution)/shard_map/ppermute | solution.py:22
  58.5 2.5 %collective-permute-done.7 = f32[4,2,70,3]{2,3,0,1:T(4,128)S(1)} collective-permute-done((f32[4,2,70,3]{2,3,0,1:T(4,128)S(1)}, f32[4,2,70,3]{2,3,0,1:T(4,128)S(1)}, u32[]{:S(2)}, u32[]{:S(2)}) %collective-permute-start.7) | collective-permute-done | bytes 6752 | tf_op jit(solution)/shard_map/ppermute | solution.py:22
  61.0 0.4 multiply_multiply_fusion.2
  61.7 0.5 fusion.139
  62.2 0.5 fusion.121
  63.5 0.5 fusion.105
  63.9 0.5 fusion.87
  65.4 0.4 fusion.204
  65.8 0.4 fusion.187
  66.2 0.6 subtract_multiply_fusion
  67.1 1.3 %collective-permute-start.8 = (f32[4,2,3,128]{2,3,0,1:T(8,128)S(1)}, f32[4,2,3,128]{2,3,0,1:T(8,128)S(1)}, u32[]{:S(2)}, u32[]{:S(2)}) collective-permute-start(f32[4,2,3,128]{2,3,0,1:T(8,128)S(1)} %get-tuple-element.43), channel_id=1, source_target_pairs={{0,8},{8,16},{16,24},{1,9},{9,17},{17,25},{2,10},{10,18},{18,26},{... | collective-permute-start | bytes 36872 | tf_op jit(solution)/shard_map/ppermute | solution.py:21
  68.4 1.3 %collective-permute-start.9 = (f32[4,2,3,128]{2,3,0,1:T(8,128)S(1)}, f32[4,2,3,128]{2,3,0,1:T(8,128)S(1)}, u32[]{:S(2)}, u32[]{:S(2)}) collective-permute-start(f32[4,2,3,128]{2,3,0,1:T(8,128)S(1)} %get-tuple-element.44), channel_id=1, source_target_pairs={{8,0},{16,8},{24,16},{9,1},{17,9},{25,17},{10,2},{18,10},{26,18},{... | collective-permute-start | bytes 36872 | tf_op jit(solution)/shard_map/ppermute | solution.py:22
  69.7 8.8 %collective-permute-done.8 = f32[4,2,3,128]{2,3,0,1:T(8,128)S(1)} collective-permute-done((f32[4,2,3,128]{2,3,0,1:T(8,128)S(1)}, f32[4,2,3,128]{2,3,0,1:T(8,128)S(1)}, u32[]{:S(2)}, u32[]{:S(2)}) %collective-permute-start.8) | collective-permute-done | bytes 12320 | tf_op jit(solution)/shard_map/ppermute | solution.py:21
  78.5 11.4 %collective-permute-done.9 = f32[4,2,3,128]{2,3,0,1:T(8,128)S(1)} collective-permute-done((f32[4,2,3,128]{2,3,0,1:T(8,128)S(1)}, f32[4,2,3,128]{2,3,0,1:T(8,128)S(1)}, u32[]{:S(2)}, u32[]{:S(2)}) %collective-permute-start.9) | collective-permute-done | bytes 12320 | tf_op jit(solution)/shard_map/ppermute | solution.py:22
  90.0 3.6 %collective-permute-start.10 = (f32[4,2,70,3]{2,3,0,1:T(4,128)S(1)}, f32[4,2,70,3]{2,3,0,1:T(4,128)S(1)}, u32[]{:S(2)}, u32[]{:S(2)}) collective-permute-start(f32[4,2,70,3]{2,3,0,1:T(4,128)S(1)} %get-tuple-element.22), channel_id=1, source_target_pairs={{0,1},{1,2},{2,3},{3,4},{4,5},{5,6},{6,7},{8,9},{9,10},{10,11},{11... | collective-permute-start | bytes 20168 | tf_op jit(solution)/shard_map/ppermute | solution.py:21
  93.6 2.1 %collective-permute-start.11 = (f32[4,2,70,3]{2,3,0,1:T(4,128)S(1)}, f32[4,2,70,3]{2,3,0,1:T(4,128)S(1)}, u32[]{:S(2)}, u32[]{:S(2)}) collective-permute-start(f32[4,2,70,3]{2,3,0,1:T(4,128)S(1)} %get-tuple-element.23), channel_id=1, source_target_pairs={{1,0},{2,1},{3,2},{4,3},{5,4},{6,5},{7,6},{9,8},{10,9},{11,10},{12... | collective-permute-start | bytes 20168 | tf_op jit(solution)/shard_map/ppermute | solution.py:22
  95.7 2.9 %collective-permute-done.11 = f32[4,2,70,3]{2,3,0,1:T(4,128)S(1)} collective-permute-done((f32[4,2,70,3]{2,3,0,1:T(4,128)S(1)}, f32[4,2,70,3]{2,3,0,1:T(4,128)S(1)}, u32[]{:S(2)}, u32[]{:S(2)}) %collective-permute-start.11) | collective-permute-done | bytes 6752 | tf_op jit(solution)/shard_map/ppermute | solution.py:22
  98.7 0.4 multiply_multiply_fusion.1
  99.5 0.5 fusion.69
  99.9 0.5 fusion.51
  101.4 0.5 fusion.35
  101.9 0.5 fusion.17
  103.3 0.4 fusion.172
  103.8 0.4 fusion.155
  104.2 0.7 fusion.5
  104.8 1.3 %collective-permute-start.12 = (f32[1,128]{0,1:T(8,128)S(1)}, f32[1,128]{0,1:T(8,128)S(1)}, u32[]{:S(2)}, u32[]{:S(2)}) collective-permute-start(f32[1,128]{0,1:T(8,128)S(1)} %bitcast.71), channel_id=1, source_target_pairs={{8,0},{16,8},{24,16},{9,1},{17,9},{25,17},{10,2},{18,10},{26,18},{... | collective-permute-start | bytes 1544 | tf_op jit(solution)/shard_map/ppermute | solution.py:30
  106.1 3.7 %collective-permute-done.12 = f32[1,128]{0,1:T(8,128)S(1)} collective-permute-done((f32[1,128]{0,1:T(8,128)S(1)}, f32[1,128]{0,1:T(8,128)S(1)}, u32[]{:S(2)}, u32[]{:S(2)}) %collective-permute-start.12) | collective-permute-done | bytes 544 | tf_op jit(solution)/shard_map/ppermute | solution.py:30
  110.0 1.9 %collective-permute-start.13 = (f32[64,1]{0,1:T(1,128)S(1)}, f32[64,1]{0,1:T(1,128)S(1)}, u32[]{:S(2)}, u32[]{:S(2)}) collective-permute-start(f32[64,1]{0,1:T(1,128)S(1)} %slice.1223), channel_id=1, source_target_pairs={{1,0},{2,1},{3,2},{4,3},{5,4},{6,5},{7,6},{9,8},{10,9},{11,10},{12... | collective-permute-start | bytes 776 | tf_op jit(solution)/shard_map/ppermute | solution.py:30
  111.9 0.9 copy.72
  112.8 2.0 %collective-permute-done.13 = f32[64,1]{0,1:T(1,128)S(1)} collective-permute-done((f32[64,1]{0,1:T(1,128)S(1)}, f32[64,1]{0,1:T(1,128)S(1)}, u32[]{:S(2)}, u32[]{:S(2)}) %collective-permute-start.13) | collective-permute-done | bytes 288 | tf_op jit(solution)/shard_map/ppermute | solution.py:30
  114.9 0.7 copy.73
  (77 shorter events, 7.2 us)
Async XLA Ops:
  1.5 0.8 copy-start.1
  2.2 0.8 copy-start.2
  3.0 0.8 copy-start.3
  3.9 5.4 %copy-start = (f32[4,2,64,128]{3,2,1,0:T(8,128)S(1)}, f32[4,2,64,128]{3,2,1,0:T(8,128)}, u32[]{:S(2)}) copy-start(f32[4,2,64,128]{3,2,1,0:T(8,128)} %param.6) | copy-start | bytes 786436
  4.0 7.5 %collective-permute-start = (f32[3,4,128]{1,2,0:T(8,128)S(1)}, f32[3,4,128]{1,2,0:T(8,128)S(1)}, u32[]{:S(2)}, u32[]{:S(2)}) collective-permute-start(f32[3,4,128]{1,2,0:T(8,128)S(1)} %get-tuple-element.50), channel_id=1, source_target_pairs={{0,8},{8,16},{16,24},{1,9},{9,17},{17,25},{2,10},{10,18},{18,26},{... | collective-permute-start | bytes 18440 | tf_op jit(solution)/shard_map/ppermute | solution.py:21
  8.0 9.7 %collective-permute-start.1 = (f32[3,4,128]{1,2,0:T(8,128)S(1)}, f32[3,4,128]{1,2,0:T(8,128)S(1)}, u32[]{:S(2)}, u32[]{:S(2)}) collective-permute-start(f32[3,4,128]{1,2,0:T(8,128)S(1)} %get-tuple-element.51), channel_id=1, source_target_pairs={{8,0},{16,8},{24,16},{9,1},{17,9},{25,17},{10,2},{18,10},{26,18},{... | collective-permute-start | bytes 18440 | tf_op jit(solution)/shard_map/ppermute | solution.py:22
  17.8 13.2 %collective-permute-start.2 = (f32[3,72,4]{1,2,0:T(4,128)S(1)}, f32[3,72,4]{1,2,0:T(4,128)S(1)}, u32[]{:S(2)}, u32[]{:S(2)}) collective-permute-start(f32[3,72,4]{1,2,0:T(4,128)S(1)} %get-tuple-element.26), channel_id=1, source_target_pairs={{0,1},{1,2},{2,3},{3,4},{4,5},{5,6},{6,7},{8,9},{9,10},{10,11},{11... | collective-permute-start | bytes 10376 | tf_op jit(solution)/shard_map/ppermute | solution.py:21
  22.4 8.5 %collective-permute-start.3 = (f32[3,72,4]{1,2,0:T(4,128)S(1)}, f32[3,72,4]{1,2,0:T(4,128)S(1)}, u32[]{:S(2)}, u32[]{:S(2)}) collective-permute-start(f32[3,72,4]{1,2,0:T(4,128)S(1)} %get-tuple-element.27), channel_id=1, source_target_pairs={{1,0},{2,1},{3,2},{4,3},{5,4},{6,5},{7,6},{9,8},{10,9},{11,10},{12... | collective-permute-start | bytes 10376 | tf_op jit(solution)/shard_map/ppermute | solution.py:22
  25.3 13.2 %collective-permute-start.4 = (f32[4,2,3,128]{2,3,0,1:T(8,128)}, f32[4,2,3,128]{2,3,0,1:T(8,128)S(1)}, u32[]{:S(2)}, u32[]{:S(2)}) collective-permute-start(f32[4,2,3,128]{2,3,0,1:T(8,128)} %get-tuple-element.45), channel_id=1, source_target_pairs={{0,8},{8,16},{16,24},{1,9},{9,17},{17,25},{2,10},{10,18},{18,26},{... | collective-permute-start | bytes 36872 | tf_op jit(solution)/shard_map/ppermute | solution.py:21
  28.5 21.3 %collective-permute-start.5 = (f32[4,2,3,128]{2,3,0,1:T(8,128)S(1)}, f32[4,2,3,128]{2,3,0,1:T(8,128)S(1)}, u32[]{:S(2)}, u32[]{:S(2)}) collective-permute-start(f32[4,2,3,128]{2,3,0,1:T(8,128)S(1)} %get-tuple-element.46), channel_id=1, source_target_pairs={{8,0},{16,8},{24,16},{9,1},{17,9},{25,17},{10,2},{18,10},{26,18},{... | collective-permute-start | bytes 36872 | tf_op jit(solution)/shard_map/ppermute | solution.py:22
  49.9 8.6 %collective-permute-start.6 = (f32[4,2,70,3]{2,3,0,1:T(4,128)S(1)}, f32[4,2,70,3]{2,3,0,1:T(4,128)S(1)}, u32[]{:S(2)}, u32[]{:S(2)}) collective-permute-start(f32[4,2,70,3]{2,3,0,1:T(4,128)S(1)} %get-tuple-element.24), channel_id=1, source_target_pairs={{0,1},{1,2},{2,3},{3,4},{4,5},{5,6},{6,7},{8,9},{9,10},{10,11},{11... | collective-permute-start | bytes 20168 | tf_op jit(solution)/shard_map/ppermute | solution.py:21
  56.0 5.1 %collective-permute-start.7 = (f32[4,2,70,3]{2,3,0,1:T(4,128)S(1)}, f32[4,2,70,3]{2,3,0,1:T(4,128)S(1)}, u32[]{:S(2)}, u32[]{:S(2)}) collective-permute-start(f32[4,2,70,3]{2,3,0,1:T(4,128)S(1)} %get-tuple-element.25), channel_id=1, source_target_pairs={{1,0},{2,1},{3,2},{4,3},{5,4},{6,5},{7,6},{9,8},{10,9},{11,10},{12... | collective-permute-start | bytes 20168 | tf_op jit(solution)/shard_map/ppermute | solution.py:22
  67.1 11.4 %collective-permute-start.8 = (f32[4,2,3,128]{2,3,0,1:T(8,128)S(1)}, f32[4,2,3,128]{2,3,0,1:T(8,128)S(1)}, u32[]{:S(2)}, u32[]{:S(2)}) collective-permute-start(f32[4,2,3,128]{2,3,0,1:T(8,128)S(1)} %get-tuple-element.43), channel_id=1, source_target_pairs={{0,8},{8,16},{16,24},{1,9},{9,17},{17,25},{2,10},{10,18},{18,26},{... | collective-permute-start | bytes 36872 | tf_op jit(solution)/shard_map/ppermute | solution.py:21
  68.4 21.5 %collective-permute-start.9 = (f32[4,2,3,128]{2,3,0,1:T(8,128)S(1)}, f32[4,2,3,128]{2,3,0,1:T(8,128)S(1)}, u32[]{:S(2)}, u32[]{:S(2)}) collective-permute-start(f32[4,2,3,128]{2,3,0,1:T(8,128)S(1)} %get-tuple-element.44), channel_id=1, source_target_pairs={{8,0},{16,8},{24,16},{9,1},{17,9},{25,17},{10,2},{18,10},{26,18},{... | collective-permute-start | bytes 36872 | tf_op jit(solution)/shard_map/ppermute | solution.py:22
  90.0 5.7 %collective-permute-start.10 = (f32[4,2,70,3]{2,3,0,1:T(4,128)S(1)}, f32[4,2,70,3]{2,3,0,1:T(4,128)S(1)}, u32[]{:S(2)}, u32[]{:S(2)}) collective-permute-start(f32[4,2,70,3]{2,3,0,1:T(4,128)S(1)} %get-tuple-element.22), channel_id=1, source_target_pairs={{0,1},{1,2},{2,3},{3,4},{4,5},{5,6},{6,7},{8,9},{9,10},{10,11},{11... | collective-permute-start | bytes 20168 | tf_op jit(solution)/shard_map/ppermute | solution.py:21
  93.6 5.1 %collective-permute-start.11 = (f32[4,2,70,3]{2,3,0,1:T(4,128)S(1)}, f32[4,2,70,3]{2,3,0,1:T(4,128)S(1)}, u32[]{:S(2)}, u32[]{:S(2)}) collective-permute-start(f32[4,2,70,3]{2,3,0,1:T(4,128)S(1)} %get-tuple-element.23), channel_id=1, source_target_pairs={{1,0},{2,1},{3,2},{4,3},{5,4},{6,5},{7,6},{9,8},{10,9},{11,10},{12... | collective-permute-start | bytes 20168 | tf_op jit(solution)/shard_map/ppermute | solution.py:22
  104.8 5.0 %collective-permute-start.12 = (f32[1,128]{0,1:T(8,128)S(1)}, f32[1,128]{0,1:T(8,128)S(1)}, u32[]{:S(2)}, u32[]{:S(2)}) collective-permute-start(f32[1,128]{0,1:T(8,128)S(1)} %bitcast.71), channel_id=1, source_target_pairs={{8,0},{16,8},{24,16},{9,1},{17,9},{25,17},{10,2},{18,10},{26,18},{... | collective-permute-start | bytes 1544 | tf_op jit(solution)/shard_map/ppermute | solution.py:30
  110.0 4.9 %collective-permute-start.13 = (f32[64,1]{0,1:T(1,128)S(1)}, f32[64,1]{0,1:T(1,128)S(1)}, u32[]{:S(2)}, u32[]{:S(2)}) collective-permute-start(f32[64,1]{0,1:T(1,128)S(1)} %slice.1223), channel_id=1, source_target_pairs={{1,0},{2,1},{3,2},{4,3},{5,4},{6,5},{7,6},{9,8},{10,9},{11,10},{12... | collective-permute-start | bytes 776 | tf_op jit(solution)/shard_map/ppermute | solution.py:30
where the time goes:
time: 116 us
  waiting for transfers between devices  57.2 us (49%)
  starting transfers between devices  35.7 us (31%)
  other arithmetic  12.5 us (11%)
  local copies, waits for them, and re-layouts  8.74 us (8%)
  between operations  1.39 us (1%)
    ppermute x6, waiting for transfers between devices, extended_2(): after = lax.ppermute(initial, axis, down)  34.3 us
    ppermute x6, starting transfers between devices, extended_2(): before = lax.ppermute(last, axis, up)  22.7 us
    ppermute x6, waiting for transfers between devices, extended_2(): before = lax.ppermute(last, axis, up)  17.2 us
    ppermute x6, starting transfers between devices, extended_2(): after = lax.ppermute(initial, axis, down)  9.82 us
    unnamed x17, local copies, waits for them, and re-layouts  6.14 us
    ppermute x2, waiting for transfers between devices, shifted(): return lax.ppermute(block, axis, route)  5.75 us
    another operation x12, other arithmetic, stencil_apply(): return jnp.stack([image_u, image_v], axis=1)  5.33 us
    ppermute x2, starting transfers between devices, shifted(): return lax.ppermute(block, axis, route)  3.21 us
  transfers between devices with their start and end apart: 14, of which 10 were waited for; matrix products, arithmetic and copies ran while one was open for 4% of the time, Pallas kernels for 0%

commit v1 on v0

v1 whole, which is shorter than its diff:
```python
import jax
import jax.numpy as jnp
from jax import lax
from jax.experimental import pallas as pl
from jax.experimental.pallas import tpu as pltpu
from jax.sharding import PartitionSpec as P

SWEEPS = 3
UPPER_BOUND = 2.4
LOWER_BOUND = 0.05
FREE_DRAG = 4.0
HALO = 8
LANES = 128
EP = 4
NCOEF = 20
MESH = pl.DeviceIdType.MESH
DIRS = ((-1, 0), (1, 0), (0, -1), (0, 1), (-1, -1), (-1, 1), (1, -1), (1, 1))


def chebyshev_weights():
    centre = 0.5 * (UPPER_BOUND + LOWER_BOUND)
    half = 0.5 * (UPPER_BOUND - LOWER_BOUND)
    ratio = centre / half
    now = 1.0 / ratio
    pairs = []
    for _ in range(SWEEPS):
        following = 1.0 / (2.0 * ratio - now)
        pairs.append((following * now, 2.0 * following / half))
        now = following
    return 1.0 / centre, pairs


def kernel(rows, forcing, observed, visc, fric, mask, dirich, vel_out, grad_out,
           F, O, K, FM, IM, DM, PK, PS, E, FRV, KF, D, R, X, B2, VO, PD, PT, GO,
           lsem, osem, ssem, rsem):
    gx, gy = lax.axis_index("gx"), lax.axis_index("gy")
    nx, ny = lax.axis_size("gx"), lax.axis_size("gy")
    ext = rows + 2 * HALO
    tiles = ext // 8
    own_tiles = rows // 8
    end = rows + HALO

    def has(dx, dy):
        cond = None
        for idx, size, step in ((gx, nx, dx), (gy, ny, dy)):
            if step:
                here = idx > 0 if step < 0 else idx < size - 1
                cond = here if cond is None else jnp.logical_and(cond, here)
        return cond

    def lacks(dx, dy):
        return jnp.logical_not(has(dx, dy))

    loads = [
        pltpu.make_async_copy(visc, K.at[0, pl.ds(HALO, rows)], lsem.at[0]),
        pltpu.make_async_copy(fric, FM, lsem.at[1]),
        pltpu.make_async_copy(mask, IM, lsem.at[2]),
        pltpu.make_async_copy(dirich, DM, lsem.at[3]),
        pltpu.make_async_copy(forcing, F.at[:, :, pl.ds(HALO, rows)], lsem.at[4]),
        pltpu.make_async_copy(observed, O.at[:, :, pl.ds(HALO, rows)], lsem.at[5]),
    ]
    for copy in loads:
        copy.start()

    barrier = pltpu.get_barrier_semaphore()
    for dx, dy in DIRS:
        @pl.when(has(dx, dy))
        def _():
            pl.semaphore_signal(barrier, inc=1, device_id=(gx + dx, gy + dy), device_id_type=MESH)

    lane = lax.broadcasted_iota(jnp.int32, (8, LANES), 1)
    low8 = (lane & 8) == 0
    left = lane < 64
    zero = jnp.zeros((8, LANES), jnp.float32)

    def roll(v, k):
        k = k % LANES
        return pltpu.roll(v, k, axis=1) if k else v

    for dx in (-1, 1):
        edge = pl.ds(0, 8) if dx < 0 else pl.ds(end, 8)

        @pl.when(lacks(dx, 0))
        def _():
            for t in range(EP):
                for c in range(2):
                    F[t, c, edge] = zero
                    O[t, c, edge] = zero
            for k in range(3):
                K[k, edge] = zero
        for dy in (-1, 1):
            @pl.when(lacks(dx, dy))
            def _():
                for k in range(3):
                    PS[0 if dy < 0 else 1, k, edge] = zero
    for dy in (-1, 1):
        @pl.when(lacks(0, dy))
        def _():
            PS[0 if dy < 0 else 1, :, pl.ds(HALO, rows)] = jnp.zeros((3, rows, LANES), jnp.float32)
    for m in range(2):
        for k in range(2):
            E[m, k, pl.ds(0, 8)] = zero
            E[m, k, pl.ds(ext + 8, 8)] = zero
    for b in range(2):
        for t in range(EP + 1):
            for c in range(2):
                for s in range(3):
                    D[b, t, c, s, pl.ds(0, 8)] = zero
                    D[b, t, c, s, pl.ds(ext + 8, 8)] = zero

    count = (1 + (gx > 0).astype(jnp.int32) + (gx < nx - 1).astype(jnp.int32)) * (
        1 + (gy > 0).astype(jnp.int32) + (gy < ny - 1).astype(jnp.int32)) - 1
    pl.semaphore_wait(barrier, count)

    def descs(d, stage):
        dx, dy = DIRS[d]
        target = (gx + dx, gy + dy)
        if dx == 0:
            src, dst = pl.ds(HALO, rows), pl.ds(HALO, rows)
        elif dx < 0:
            src, dst = pl.ds(HALO, 8), pl.ds(end, 8)
        else:
            src, dst = pl.ds(rows, 8), pl.ds(0, 8)
        if dy == 0:
            if stage == 0:
                pairs = [(0, F.at[:, :, src], F.at[:, :, dst]), (1, K.at[:, src], K.at[:, dst])]
            else:
                pairs = [(2, O.at[:, :, src], O.at[:, :, dst])]
        else:
            side = 0 if dy > 0 else 1
            part = pl.ds(0, 2) if stage == 0 else pl.ds(2, 1)
            pairs = [(0 if stage == 0 else 2, PK.at[part, src], PS.at[side, part, dst])]
        return [
            (j, pltpu.make_async_remote_copy(
                src_ref=s, dst_ref=q, send_sem=ssem.at[d, j], recv_sem=rsem.at[d, j],
                device_id=target, device_id_type=MESH))
            for j, s, q in pairs
        ]

    def send(d, stage, only=None):
        @pl.when(has(*DIRS[d]))
        def _():
            for j, copy in descs(d, stage):
                if only is None or j == only:
                    copy.start()

    def receive(d, stage):
        dx, dy = DIRS[d]

        @pl.when(has(-dx, -dy))
        def _():
            for _, copy in descs(d, stage):
                copy.wait_recv()

    def sent(d, stage):
        @pl.when(has(*DIRS[d]))
        def _():
            for _, copy in descs(d, stage):
                copy.wait_send()

    def at(r, off=0):
        return pl.ds(pl.multiple_of(r * 8, 8) + off, 8)

    def pack(get):
        out = None
        for t in range(EP):
            for c in range(2):
                g = c * EP + t
                v = roll(get(t, c), 16 * g + 8)
                out = v if out is None else jnp.where((lane >> 4) == g, v, out)
        return out

    def pack_coef(r):
        out = roll(K[0, at(r)], 8)
        out = jnp.where((lane >> 4) == 1, roll(K[1, at(r)], 24), out)
        return jnp.where((lane >> 4) == 2, roll(K[2, at(r)], 40), out)

    for copy in loads[:5]:
        copy.wait()
    for d in (0, 1):
        send(d, 0, 0)

    @pl.loop(0, own_tiles)
    def _(r):
        m = IM[at(r)]
        drag = jnp.where(m == 2, FM[at(r)], jnp.where(m == 0, FREE_DRAG, 0.0))
        K[1, at(r + 1)] = drag
        K[2, at(r + 1)] = (1 - DM[at(r)]).astype(jnp.float32)

    for d in (0, 1):
        send(d, 0, 1)

    @pl.loop(1, own_tiles + 1)
    def _(r):
        PK[0, at(r)] = pack(lambda t, c: F[t, c, at(r)])
        PK[1, at(r)] = pack_coef(r)

    for d in range(2, 8):
        send(d, 0)
    loads[5].wait()
    for d in (0, 1):
        send(d, 1)

    @pl.loop(1, own_tiles + 1)
    def _(r):
        PK[2, at(r)] = pack(lambda t, c: O[t, c, at(r)])

    for d in range(2, 8):
        send(d, 1)

    for d in range(8):
        receive(d, 0)

    def strips(k, r, own):
        sl = jnp.where(low8, PS[0, k, at(r)], own)
        sr = jnp.where(low8, own, PS[1, k, at(r)])
        return sl, sr

    def spread(sl, sr):
        return jnp.where(left, sl, roll(sr, 64)), jnp.where(left, roll(sl, 64), sr)

    @pl.loop(0, tiles)
    def _(r):
        E[0, 0, at(r, 8)] = K[0, at(r)]
        E[0, 1, at(r, 8)] = K[1, at(r)]
        sl, sr = strips(1, r, pack_coef(r))
        for k in range(3):
            v = jnp.where(lane < 16, roll(sl, -16 * k),
                          jnp.where((lane >> 4) == 4, roll(sr, 64 - 16 * k), 0.0))
            v = v + roll(v, 16)
            v = v + roll(v, 32)
            if k < 2:
                E[1, k, at(r, 8)] = v
            else:
                FRV[at(r)] = v

    first_scale, weights = chebyshev_weights()

    @pl.loop(0, tiles)
    def _(r):
        for m in range(2):
            e0 = E[m, 0, at(r, 8)]
            en = E[m, 0, at(r, 9)]
            es = E[m, 0, at(r, 7)]
            ee = roll(e0, -1)
            ew = roll(e0, 1)
            q = E[m, 1, at(r, 8)] + E[m, 1, at(r, 7)]
            drag = 0.25 * (q + roll(q, 1))
            free = K[2, at(r)] if m == 0 else FRV[at(r)]
            ap, am = 0.5 * (e0 + en), 0.5 * (e0 + es)
            bp, bm = 0.5 * (e0 + ee), 0.5 * (e0 + ew)
            asum, bsum = ap + am, bp + bm
            du = 4.0 * asum + bsum + drag
            dv = asum + 4.0 * bsum + drag
            n2, n4, s2, s4 = 0.5 * en, 0.25 * en, 0.5 * es, 0.25 * es
            e2, e4, w2, w4 = 0.5 * ee, 0.25 * ee, 0.5 * ew, 0.25 * ew
            vals = (
                du, 4.0 * ap, 4.0 * am, bp, bm, n2 + e4, n2 + w4, s2 + e4, s2 + w4,
                free / (du + 1.0 - free),
                dv, ap, am, 4.0 * bp, 4.0 * bm, n4 + e2, n4 + w2, s4 + e2, s4 + w2,
                free / (dv + 1.0 - free),
            )
            for k, v in enumerate(vals):
                KF[m, k, at(r)] = v

    def put(buf, t, c, r, d):
        D[buf, t, c, 0, at(r, 8)] = d
        D[buf, t, c, 1, at(r, 8)] = roll(d, -1)
        D[buf, t, c, 2, at(r, 8)] = roll(d, 1)

    def begin(t, r, iv, b):
        for c in range(2):
            d = iv[c] * b[c] * first_scale
            R[t, c, at(r)] = b[c]
            X[t, c, at(r)] = d
            put(0, t, c, r, d)

    def sweep(k, lo, hi):
        src, dst = k % 2, 1 - k % 2
        wa, wb = weights[k]
        last = k == SWEEPS - 1

        @pl.loop(lo, hi)
        def _(r):
            for t in range(EP + 1):
                m = 0 if t < EP else 1
                cf = lambda i: KF[m, i, at(r)]
                w = [[[D[src, t, c, s, at(r, 8 + o)] for o in (0, 1, -1)] for s in range(3)]
                     for c in range(2)]
                for c in range(2):
                    a, x = w[c], w[1 - c]
                    o = 10 * c
                    res = R[t, c, at(r)]
                    p1 = cf(o + 1) * a[0][1] + cf(o + 2) * a[0][2]
                    p2 = cf(o + 3) * a[1][0] + cf(o + 4) * a[2][0]
                    p3 = cf(o + 5) * x[1][1] - cf(o + 6) * x[2][1]
                    p4 = cf(o + 8) * x[2][2] - cf(o + 7) * x[1][2]
                    res = (res - cf(o) * a[0][0]) + ((p1 + p2) + (p3 + p4))
                    d = wa * a[0][0] + wb * (cf(o + 9) * res)
                    X[t, c, at(r)] = X[t, c, at(r)] + d
                    if not last:
                        R[t, c, at(r)] = res
                        put(dst, t, c, r, d)

    @pl.loop(0, tiles)
    def _(r):
        iv = [[KF[m, 9, at(r)], KF[m, 19, at(r)]] for m in range(2)]
        free = K[2, at(r)]
        for t in range(EP):
            begin(t, r, iv[0], [free * F[t, c, at(r)] for c in range(2)])
        u, v = spread(*strips(0, r, pack(lambda t, c: F[t, c, at(r)])))
        fr = FRV[at(r)]
        begin(EP, r, iv[1], [fr * u, fr * v])

    for k in range(SWEEPS):
        sweep(k, 0, tiles)

    for d in range(8):
        receive(d, 1)

    near, far = lane < 4, lane >= LANES - 4

    @pl.loop(0, tiles)
    def _(r):
        iv = [[KF[m, 9, at(r)], KF[m, 19, at(r)]] for m in range(2)]
        free = K[2, at(r)]
        side = [X[EP, c, at(r)] for c in range(2)]
        vel = [[None, None] for _ in range(EP)]
        for t in range(EP):
            for c in range(2):
                x = X[t, c, at(r)]
                x = jnp.where(near, roll(side[c], -16 * t - 8), x)
                x = jnp.where(far, roll(side[c], 56 - 16 * t), x)
                vel[t][c] = x
                VO[t, c, at(r)] = x
        p = pack(lambda t, c: vel[t][c])
        own = spread(p, p)
        mine = low8 != left
        obs = spread(*strips(2, r, pack(lambda t, c: O[t, c, at(r)])))
        fr = FRV[at(r)]
        sv = [jnp.where(mine, own[c], side[c]) for c in range(2)]
        for c in range(2):
            B2[c, at(r)] = sv[c]
        for t in range(EP):
            begin(t, r, iv[0], [free * (vel[t][c] - O[t, c, at(r)]) for c in range(2)])
        begin(EP, r, iv[1], [fr * (sv[c] - obs[c]) for c in range(2)])

    out_copy = pltpu.make_async_copy(VO.at[:, :, pl.ds(HALO, rows)], vel_out, osem.at[0])
    out_copy.start()

    for k in range(SWEEPS):
        sweep(k, 0 if k < SWEEPS - 1 else 1, tiles)

    @pl.loop(1, tiles)
    def _(r):
        p = None
        for t in range(EP):
            for c in range(2):
                q = X[t, c, at(r)] * VO[t, c, at(r)]
                p = q if p is None else p + q
        s = X[EP, 0, at(r)] * B2[0, at(r)] + X[EP, 1, at(r)] * B2[1, at(r)]
        s = s + roll(s, 16)
        s = s + roll(s, 32)
        p = jnp.where(near, roll(s, -56), p)
        p = jnp.where(far, roll(s, 8), p)
        nxt = jnp.where(lane == LANES - 1, roll(s, 7), roll(p, -1))
        PD[at(r)] = p + nxt

    @pl.loop(0, own_tiles)
    def _(r):
        q = PD[at(r, 8)] + PD[at(r, 9)]
        GO[at(r)] = jnp.where(IM[at(r)] == 2, -0.25 * q, 0.0)

    grad_copy = pltpu.make_async_copy(GO, grad_out, osem.at[1])
    grad_copy.start()
    for d in range(8):
        sent(d, 0)
        sent(d, 1)
    out_copy.wait()
    grad_copy.wait()


def body(forcing, observed, viscosity, friction, ice_mask, dirichlet):
    rows = viscosity.shape[0]
    ext = rows + 2 * HALO
    f32 = jnp.float32
    V = pltpu.VMEM
    grid = (rows, LANES)
    velocity, gradient = pl.pallas_call(
        lambda *refs: kernel(rows, *refs),
        out_shape=(
            jax.ShapeDtypeStruct(forcing.shape, f32),
            jax.ShapeDtypeStruct(grid, f32),
        ),
        in_specs=[pl.BlockSpec(memory_space=pl.ANY)] * 6,
        out_specs=(pl.BlockSpec(memory_space=pl.ANY),) * 2,
        scratch_shapes=[
            V((EP, 2, ext, LANES), f32),
            V((EP, 2, ext, LANES), f32),
            V((3, ext, LANES), f32),
            V(grid, f32), V(grid, jnp.int32), V(grid, jnp.int32),
            V((3, ext, LANES), f32),
            V((2, 3, ext, LANES), f32),
            V((2, 2, ext + 16, LANES), f32),
            V((ext, LANES), f32),
            V((2, NCOEF, ext, LANES), f32),
            V((2, EP + 1, 2, 3, ext + 16, LANES), f32),
            V((EP + 1, 2, ext, LANES), f32),
            V((EP + 1, 2, ext, LANES), f32),
            V((2, ext, LANES), f32),
            V((EP, 2, ext, LANES), f32),
            V((ext, LANES), f32),
            V((8, LANES), f32),
            V(grid, f32),
            pltpu.SemaphoreType.DMA((6,)),
            pltpu.SemaphoreType.DMA((2,)),
            pltpu.SemaphoreType.DMA((8, 3)),
            pltpu.SemaphoreType.DMA((8, 3)),
        ],
        compiler_params=pltpu.CompilerParams(
            collective_id=0, has_side_effects=True, vmem_limit_bytes=24 * 1024 * 1024
        ),
        cost_estimate=pl.CostEstimate(flops=40_000_000, bytes_accessed=1_000_000, transcendentals=0),
    )(forcing, observed, viscosity, friction, ice_mask, dirichlet)
    return velocity, gradient


def solution(mesh):
    wide, flat = P(None, None, "gx", "gy"), P("gx", "gy")
    return jax.shard_map(
        body,
        mesh=mesh,
        in_specs=(wide, wide, flat, flat, flat, flat),
        out_specs=(wide, flat),
        check_vma=False,
    )
```

time: 116 us -> 34.1 us (0.29)
  the two profiles are of different devices: /device:TPU:1 before, /device:TPU:0 now
where the time goes in v1:
time: 34.1 us; the launch traced here: 33.7 us
  Pallas kernels  26.8 us (79%)
  local copies, waits for them, and re-layouts  6.24 us (18%)
  between operations  0.65 us (2%)
    pallas_call x1, Pallas kernels, body(): pl.pallas_call(lambda *refs: kernel(rows, *refs), out_shape=(jax.ShapeDty...  26.8 us
    unnamed x14, local copies, waits for them, and re-layouts  6.24 us

profile of v1, /device:TPU:0, one launch (start us, length us, event | category | flops | bytes accessed | tf_op | source)
XLA Modules:
  0.0 33.7 jit_solution(8683895702918193034)
XLA Ops:
  0.6 0.0 copy-start
  0.6 0.9 %copy-done = f32[4,2,64,128]{3,2,1,0:T(8,128)S(1)} copy-done((f32[4,2,64,128]{3,2,1,0:T(8,128)S(1)}, f32[4,2,64,128]{3,2,1,0:T(8,128)}, u32[]{:S(2)}) %copy-start) | copy-done | bytes 262168
  1.6 0.0 copy-start.1
  1.6 0.9 %copy-done.1 = f32[4,2,64,128]{3,2,1,0:T(8,128)S(1)} copy-done((f32[4,2,64,128]{3,2,1,0:T(8,128)S(1)}, f32[4,2,64,128]{3,2,1,0:T(8,128)}, u32[]{:S(2)}) %copy-start.1) | copy-done | bytes 262168
  2.5 0.0 copy-start.2
  2.5 0.8 %copy-done.2 = f32[64,128]{1,0:T(8,128)S(1)} copy-done((f32[64,128]{1,0:T(8,128)S(1)}, f32[64,128]{1,0:T(8,128)}, u32[]{:S(2)}) %copy-start.2) | copy-done | bytes 32792
  3.3 0.0 copy-start.3
  3.3 0.8 %copy-done.3 = f32[64,128]{1,0:T(8,128)S(1)} copy-done((f32[64,128]{1,0:T(8,128)S(1)}, f32[64,128]{1,0:T(8,128)}, u32[]{:S(2)}) %copy-start.3) | copy-done | bytes 32792
  4.0 0.0 copy-start.4
  4.1 0.8 %copy-done.4 = s32[64,128]{1,0:T(8,128)S(1)} copy-done((s32[64,128]{1,0:T(8,128)S(1)}, s32[64,128]{1,0:T(8,128)}, u32[]{:S(2)}) %copy-start.4) | copy-done | bytes 32792
  4.8 0.0 copy-start.5
  4.8 0.8 %copy-done.5 = s32[64,128]{1,0:T(8,128)S(1)} copy-done((s32[64,128]{1,0:T(8,128)S(1)}, s32[64,128]{1,0:T(8,128)}, u32[]{:S(2)}) %copy-start.5) | copy-done | bytes 32792
  5.6 26.8 %shard_map.77 = (f32[4,2,64,128]{3,2,1,0:T(8,128)S(1)}, f32[64,128]{1,0:T(8,128)S(1)}) custom-call(f32[4,2,64,128]{3,2,1,0:T(8,128)S(1)} %copy-done, f32[4,2,64,128]{3,2,1,0:T(8,128)S(1)} %copy-done.1, f32[64,128]{1,0:T(8,128)S(1)} %copy-done.2, f32[64,128]{1,0:T(8,128)S(1)} %copy-done.3, s32[64,128]{1,0:T(8,128)S(1)} %copy-done.4, s32[64,128]{1,0:T(8,128)S(1)} %copy-done.5), custom_call_target="tpu_custom_call" | custom-call | flops 40000000 | bytes 1000000 | tf_op jit(solution)/shard_map/pallas_call | solution.py:389
  32.4 0.7 %copy.10 = f32[4,2,64,128]{3,2,1,0:T(8,128)} copy(f32[4,2,64,128]{3,2,1,0:T(8,128)S(1)} %get-tuple-element.4) | data formatting | bytes 524288
  33.1 0.6 %copy.11 = f32[64,128]{1,0:T(8,128)} copy(f32[64,128]{1,0:T(8,128)S(1)} %get-tuple-element.5) | data formatting | bytes 65536
Async XLA Ops:
  0.6 1.0 %copy-start = (f32[4,2,64,128]{3,2,1,0:T(8,128)S(1)}, f32[4,2,64,128]{3,2,1,0:T(8,128)}, u32[]{:S(2)}) copy-start(f32[4,2,64,128]{3,2,1,0:T(8,128)} %refs_0_.1) | copy-start | bytes 786436
  1.6 0.9 %copy-start.1 = (f32[4,2,64,128]{3,2,1,0:T(8,128)S(1)}, f32[4,2,64,128]{3,2,1,0:T(8,128)}, u32[]{:S(2)}) copy-start(f32[4,2,64,128]{3,2,1,0:T(8,128)} %refs_1_.1) | copy-start | bytes 786436
  2.5 0.8 %copy-start.2 = (f32[64,128]{1,0:T(8,128)S(1)}, f32[64,128]{1,0:T(8,128)}, u32[]{:S(2)}) copy-start(f32[64,128]{1,0:T(8,128)} %refs_2_.1) | copy-start | bytes 98308
  3.3 0.8 %copy-start.3 = (f32[64,128]{1,0:T(8,128)S(1)}, f32[64,128]{1,0:T(8,128)}, u32[]{:S(2)}) copy-start(f32[64,128]{1,0:T(8,128)} %refs_3_.1) | copy-start | bytes 98308
  4.0 0.8 %copy-start.4 = (s32[64,128]{1,0:T(8,128)S(1)}, s32[64,128]{1,0:T(8,128)}, u32[]{:S(2)}) copy-start(s32[64,128]{1,0:T(8,128)} %refs_4_.1) | copy-start | bytes 98308
  4.8 0.8 %copy-start.5 = (s32[64,128]{1,0:T(8,128)S(1)}, s32[64,128]{1,0:T(8,128)}, u32[]{:S(2)}) copy-start(s32[64,128]{1,0:T(8,128)} %refs_5_.1) | copy-start | bytes 98308

commit v2 on v1

--- a/solution.py
+++ b/solution.py
@@ -31,7 +31,7 @@
 
 
 def kernel(rows, forcing, observed, visc, fric, mask, dirich, vel_out, grad_out,
-           F, O, K, FM, IM, DM, PK, PS, E, FRV, KF, D, R, X, B2, VO, PD, PT, GO,
+           F, O, K, FM, IM, DM, PK, PS, E, FRV, KF, D0, D1, R, X, B2, VO, PD, PT, GO,
            lsem, osem, ssem, rsem):
     gx, gy = lax.axis_index("gx"), lax.axis_index("gy")
     nx, ny = lax.axis_size("gx"), lax.axis_size("gy")
@@ -101,18 +101,18 @@
         for k in range(2):
             E[m, k, pl.ds(0, 8)] = zero
             E[m, k, pl.ds(ext + 8, 8)] = zero
-    for b in range(2):
+    for D in (D0, D1):
         for t in range(EP + 1):
             for c in range(2):
                 for s in range(3):
-                    D[b, t, c, s, pl.ds(0, 8)] = zero
-                    D[b, t, c, s, pl.ds(ext + 8, 8)] = zero
+                    D[t, c, s, pl.ds(0, 8)] = zero
+                    D[t, c, s, pl.ds(ext + 8, 8)] = zero
 
     count = (1 + (gx > 0).astype(jnp.int32) + (gx < nx - 1).astype(jnp.int32)) * (
         1 + (gy > 0).astype(jnp.int32) + (gy < ny - 1).astype(jnp.int32)) - 1
     pl.semaphore_wait(barrier, count)
 
-    def descs(d, stage):
+    def descs(d, stage, only=None):
         dx, dy = DIRS[d]
         target = (gx + dx, gy + dy)
         if dx == 0:
@@ -135,14 +135,14 @@
                 src_ref=s, dst_ref=q, send_sem=ssem.at[d, j], recv_sem=rsem.at[d, j],
                 device_id=target, device_id_type=MESH))
             for j, s, q in pairs
+            if only is None or j == only
         ]
 
     def send(d, stage, only=None):
         @pl.when(has(*DIRS[d]))
         def _():
-            for j, copy in descs(d, stage):
-                if only is None or j == only:
-                    copy.start()
+            for _, copy in descs(d, stage, only):
+                copy.start()
 
     def receive(d, stage):
         dx, dy = DIRS[d]
@@ -159,6 +159,8 @@
                 copy.wait_send()
 
     def at(r, off=0):
+        if isinstance(r, int):
+            return pl.ds(r * 8 + off, 8)
         return pl.ds(pl.multiple_of(r * 8, 8) + off, 8)
 
     def pack(get):
@@ -180,7 +182,7 @@
     for d in (0, 1):
         send(d, 0, 0)
 
-    @pl.loop(0, own_tiles)
+    @pl.loop(0, own_tiles, unroll=True)
     def _(r):
         m = IM[at(r)]
         drag = jnp.where(m == 2, FM[at(r)], jnp.where(m == 0, FREE_DRAG, 0.0))
@@ -190,7 +192,7 @@
     for d in (0, 1):
         send(d, 0, 1)
 
-    @pl.loop(1, own_tiles + 1)
+    @pl.loop(1, own_tiles + 1, unroll=True)
     def _(r):
         PK[0, at(r)] = pack(lambda t, c: F[t, c, at(r)])
         PK[1, at(r)] = pack_coef(r)
@@ -201,7 +203,7 @@
     for d in (0, 1):
         send(d, 1)
 
-    @pl.loop(1, own_tiles + 1)
+    @pl.loop(1, own_tiles + 1, unroll=True)
     def _(r):
         PK[2, at(r)] = pack(lambda t, c: O[t, c, at(r)])
 
@@ -219,7 +221,7 @@
     def spread(sl, sr):
         return jnp.where(left, sl, roll(sr, 64)), jnp.where(left, roll(sl, 64), sr)
 
-    @pl.loop(0, tiles)
+    @pl.loop(0, tiles, unroll=True)
     def _(r):
         E[0, 0, at(r, 8)] = K[0, at(r)]
         E[0, 1, at(r, 8)] = K[1, at(r)]
@@ -236,7 +238,7 @@
 
     first_scale, weights = chebyshev_weights()
 
-    @pl.loop(0, tiles)
+    @pl.loop(0, tiles, unroll=True)
     def _(r):
         for m in range(2):
             e0 = E[m, 0, at(r, 8)]
@@ -264,28 +266,29 @@
                 KF[m, k, at(r)] = v
 
     def put(buf, t, c, r, d):
-        D[buf, t, c, 0, at(r, 8)] = d
-        D[buf, t, c, 1, at(r, 8)] = roll(d, -1)
-        D[buf, t, c, 2, at(r, 8)] = roll(d, 1)
+        buf[t, c, 0, at(r, 8)] = d
+        buf[t, c, 1, at(r, 8)] = roll(d, -1)
+        buf[t, c, 2, at(r, 8)] = roll(d, 1)
 
     def begin(t, r, iv, b):
         for c in range(2):
             d = iv[c] * b[c] * first_scale
             R[t, c, at(r)] = b[c]
             X[t, c, at(r)] = d
-            put(0, t, c, r, d)
+            put(D0, t, c, r, d)
 
     def sweep(k, lo, hi):
-        src, dst = k % 2, 1 - k % 2
+        src, dst = (D0, D1) if k % 2 == 0 else (D1, D0)
         wa, wb = weights[k]
         last = k == SWEEPS - 1
 
-        @pl.loop(lo, hi)
+        @pl.loop(lo, hi, unroll=True)
         def _(r):
             for t in range(EP + 1):
-                m = 0 if t < EP else 1
-                cf = lambda i: KF[m, i, at(r)]
-                w = [[[D[src, t, c, s, at(r, 8 + o)] for o in (0, 1, -1)] for s in range(3)]
+                if t == 0 or t == EP:
+                    coef = [KF[0 if t < EP else 1, i, at(r)] for i in range(NCOEF)]
+                cf = lambda i: coef[i]
+                w = [[[src[t, c, s, at(r, 8 + o)] for o in (0, 1, -1)] for s in range(3)]
                      for c in range(2)]
                 for c in range(2):
                     a, x = w[c], w[1 - c]
@@ -302,7 +305,7 @@
                         R[t, c, at(r)] = res
                         put(dst, t, c, r, d)
 
-    @pl.loop(0, tiles)
+    @pl.loop(0, tiles, unroll=True)
     def _(r):
         iv = [[KF[m, 9, at(r)], KF[m, 19, at(r)]] for m in range(2)]
         free = K[2, at(r)]
@@ -320,7 +323,7 @@
 
     near, far = lane < 4, lane >= LANES - 4
 
-    @pl.loop(0, tiles)
+    @pl.loop(0, tiles, unroll=True)
     def _(r):
         iv = [[KF[m, 9, at(r)], KF[m, 19, at(r)]] for m in range(2)]
         free = K[2, at(r)]
@@ -351,7 +354,7 @@
     for k in range(SWEEPS):
         sweep(k, 0 if k < SWEEPS - 1 else 1, tiles)
 
-    @pl.loop(1, tiles)
+    @pl.loop(1, tiles, unroll=True)
     def _(r):
         p = None
         for t in range(EP):
@@ -366,7 +369,7 @@
         nxt = jnp.where(lane == LANES - 1, roll(s, 7), roll(p, -1))
         PD[at(r)] = p + nxt
 
-    @pl.loop(0, own_tiles)
+    @pl.loop(0, own_tiles, unroll=True)
     def _(r):
         q = PD[at(r, 8)] + PD[at(r, 9)]
         GO[at(r)] = jnp.where(IM[at(r)] == 2, -0.25 * q, 0.0)
@@ -392,8 +395,8 @@
             jax.ShapeDtypeStruct(forcing.shape, f32),
             jax.ShapeDtypeStruct(grid, f32),
         ),
-        in_specs=[pl.BlockSpec(memory_space=pl.ANY)] * 6,
-        out_specs=(pl.BlockSpec(memory_space=pl.ANY),) * 2,
+        in_specs=[pl.BlockSpec(memory_space=pltpu.HBM)] * 6,
+        out_specs=(pl.BlockSpec(memory_space=pltpu.HBM),) * 2,
         scratch_shapes=[
             V((EP, 2, ext, LANES), f32),
             V((EP, 2, ext, LANES), f32),
@@ -404,7 +407,8 @@
             V((2, 2, ext + 16, LANES), f32),
             V((ext, LANES), f32),
             V((2, NCOEF, ext, LANES), f32),
-            V((2, EP + 1, 2, 3, ext + 16, LANES), f32),
+            V((EP + 1, 2, 3, ext + 16, LANES), f32),
+            V((EP + 1, 2, 3, ext + 16, LANES), f32),
             V((EP + 1, 2, ext, LANES), f32),
             V((EP + 1, 2, ext, LANES), f32),
             V((2, ext, LANES), f32),
@@ -418,7 +422,7 @@
             pltpu.SemaphoreType.DMA((8, 3)),
         ],
         compiler_params=pltpu.CompilerParams(
-            collective_id=0, has_side_effects=True, vmem_limit_bytes=24 * 1024 * 1024
+            collective_id=0, has_side_effects=True, vmem_limit_bytes=63 * 1024 * 1024
         ),
         cost_estimate=pl.CostEstimate(flops=40_000_000, bytes_accessed=1_000_000, transcendentals=0),
     )(forcing, observed, viscosity, friction, ice_mask, dirichlet)

time: 34.1 us -> 19.9 us (0.58)
  Pallas kernels: 26.8 us -> 16.8 us
  local copies, waits for them, and re-layouts: 6.24 us -> 2.3 us
    pallas_call x1, Pallas kernels: 26.8 us -> 16.8 us  [body(): pl.pallas_call(lambda *refs: kernel(rows, *refs), out_shape=(jax.ShapeDty...]
    unnamed x14 -> x4, local copies, waits for them, and re-layouts: 6.24 us -> 2.3 us
where the time goes in v2:
time: 19.9 us; the launch traced here: 19.7 us
  Pallas kernels  16.8 us (84%)
  local copies, waits for them, and re-layouts  2.3 us (12%)
  between operations  0.65 us (3%)
    pallas_call x1, Pallas kernels, body(): pl.pallas_call(lambda *refs: kernel(rows, *refs), out_shape=(jax.ShapeDty...  16.8 us
    unnamed x4, local copies, waits for them, and re-layouts  2.3 us

profile of v2, /device:TPU:0, one launch (start us, length us, event | category | flops | bytes accessed | tf_op | source)
XLA Modules:
  0.0 19.7 jit_solution(1805030953571253168)
XLA Ops:
  0.6 16.8 %shard_map.77 = (f32[4,2,64,128]{3,2,1,0:T(8,128)}, f32[64,128]{1,0:T(8,128)}) custom-call(f32[4,2,64,128]{3,2,1,0:T(8,128)} %refs_0_.1, f32[4,2,64,128]{3,2,1,0:T(8,128)} %refs_1_.1, f32[64,128]{1,0:T(8,128)} %refs_2_.1, f32[64,128]{1,0:T(8,128)} %refs_3_.1, s32[64,128]{1,0:T(8,128)} %refs_4_.1, s32[64,128]{1,0:T(8,128)} %refs_5_.1), custom_call_target="tpu_custom_call" | custom-call | flops 40000000 | bytes 1000000 | tf_op jit(solution)/shard_map/pallas_call | solution.py:392
  17.4 0.0 copy-start
  17.4 1.7 %copy.10 = f32[4,2,64,128]{3,2,1,0:T(8,128)} copy(f32[4,2,64,128]{3,2,1,0:T(8,128)} %get-tuple-element.4) | data formatting | bytes 524288
  19.1 0.0 copy-done
  19.1 0.6 %copy.11 = f32[64,128]{1,0:T(8,128)} copy(f32[64,128]{1,0:T(8,128)S(1)} %copy-done) | data formatting | bytes 65536
Async XLA Ops:
  17.4 1.7 %copy-start = (f32[64,128]{1,0:T(8,128)S(1)}, f32[64,128]{1,0:T(8,128)}, u32[]{:S(2)}) copy-start(f32[64,128]{1,0:T(8,128)} %get-tuple-element.5) | copy-start | bytes 98308

commit v3 on v2

--- a/solution.py
+++ b/solution.py
@@ -31,8 +31,8 @@
 
 
 def kernel(rows, forcing, observed, visc, fric, mask, dirich, vel_out, grad_out,
-           F, O, K, FM, IM, DM, PK, PS, E, FRV, KF, D0, D1, R, X, B2, VO, PD, PT, GO,
-           lsem, osem, ssem, rsem):
+           F, O, K, FM, IM, DM, PK, PS, E, FRV, KF, D0, D1, R, X, B2, VO, PD, PT,
+           lsem, ssem, rsem):
     gx, gy = lax.axis_index("gx"), lax.axis_index("gy")
     nx, ny = lax.axis_size("gx"), lax.axis_size("gy")
     ext = rows + 2 * HALO
@@ -177,10 +177,11 @@
         out = jnp.where((lane >> 4) == 1, roll(K[1, at(r)], 24), out)
         return jnp.where((lane >> 4) == 2, roll(K[2, at(r)], 40), out)
 
-    for copy in loads[:5]:
-        copy.wait()
+    loads[4].wait()
     for d in (0, 1):
         send(d, 0, 0)
+    for copy in loads[:4]:
+        copy.wait()
 
     @pl.loop(0, own_tiles, unroll=True)
     def _(r):
@@ -210,9 +211,6 @@
     for d in range(2, 8):
         send(d, 1)
 
-    for d in range(8):
-        receive(d, 0)
-
     def strips(k, r, own):
         sl = jnp.where(low8, PS[0, k, at(r)], own)
         sr = jnp.where(low8, own, PS[1, k, at(r)])
@@ -221,10 +219,74 @@
     def spread(sl, sr):
         return jnp.where(left, sl, roll(sr, 64)), jnp.where(left, roll(sl, 64), sr)
 
-    @pl.loop(0, tiles, unroll=True)
-    def _(r):
+    first_scale, weights = chebyshev_weights()
+
+    def put(buf, t, c, r, d):
+        buf[t, c, 0, at(r, 8)] = d
+        buf[t, c, 1, at(r, 8)] = roll(d, -1)
+        buf[t, c, 2, at(r, 8)] = roll(d, 1)
+
+    def begin(t, r, iv, b):
+        for c in range(2):
+            d = iv[c] * b[c] * first_scale
+            R[t, c, at(r)] = b[c]
+            X[t, c, at(r)] = d
+            put(D0, t, c, r, d)
+
+    def coefs(m, r):
+        e0 = E[m, 0, at(r, 8)]
+        en = E[m, 0, at(r, 9)]
+        es = E[m, 0, at(r, 7)]
+        ee = roll(e0, -1)
+        ew = roll(e0, 1)
+        q = E[m, 1, at(r, 8)] + E[m, 1, at(r, 7)]
+        drag = 0.25 * (q + roll(q, 1))
+        free = K[2, at(r)] if m == 0 else FRV[at(r)]
+        ap, am = 0.5 * (e0 + en), 0.5 * (e0 + es)
+        bp, bm = 0.5 * (e0 + ee), 0.5 * (e0 + ew)
+        asum, bsum = ap + am, bp + bm
+        du = 4.0 * asum + bsum + drag
+        dv = asum + 4.0 * bsum + drag
+        n2, n4, s2, s4 = 0.5 * en, 0.25 * en, 0.5 * es, 0.25 * es
+        e2, e4, w2, w4 = 0.5 * ee, 0.25 * ee, 0.5 * ew, 0.25 * ew
+        vals = (
+            du, 4.0 * ap, 4.0 * am, bp, bm, n2 + e4, n2 + w4, s2 + e4, s2 + w4,
+            free / (du + 1.0 - free),
+            dv, ap, am, 4.0 * bp, 4.0 * bm, n4 + e2, n4 + w2, s4 + e2, s4 + w2,
+            free / (dv + 1.0 - free),
+        )
+        for k, v in enumerate(vals):
+            KF[m, k, at(r)] = v
+
+    def start_main(r):
+        coefs(0, r)
+        iv = [KF[0, 9, at(r)], KF[0, 19, at(r)]]
+        free = K[2, at(r)]
+        for t in range(EP):
+            begin(t, r, iv, [free * F[t, c, at(r)] for c in range(2)])
+
+    def fill_main(r):
         E[0, 0, at(r, 8)] = K[0, at(r)]
         E[0, 1, at(r, 8)] = K[1, at(r)]
+
+    @pl.loop(1, own_tiles + 1, unroll=True)
+    def _(r):
+        fill_main(r)
+
+    @pl.loop(2, own_tiles, unroll=True)
+    def _(r):
+        start_main(r)
+
+    for d in range(8):
+        receive(d, 0)
+
+    for r in (0, tiles - 1):
+        fill_main(r)
+    for r in (0, 1, tiles - 2, tiles - 1):
+        start_main(r)
+
+    @pl.loop(0, tiles, unroll=True)
+    def _(r):
         sl, sr = strips(1, r, pack_coef(r))
         for k in range(3):
             v = jnp.where(lane < 16, roll(sl, -16 * k),
@@ -236,46 +298,9 @@
             else:
                 FRV[at(r)] = v
 
-    first_scale, weights = chebyshev_weights()
-
     @pl.loop(0, tiles, unroll=True)
     def _(r):
-        for m in range(2):
-            e0 = E[m, 0, at(r, 8)]
-            en = E[m, 0, at(r, 9)]
-            es = E[m, 0, at(r, 7)]
-            ee = roll(e0, -1)
-            ew = roll(e0, 1)
-            q = E[m, 1, at(r, 8)] + E[m, 1, at(r, 7)]
-            drag = 0.25 * (q + roll(q, 1))
-            free = K[2, at(r)] if m == 0 else FRV[at(r)]
-            ap, am = 0.5 * (e0 + en), 0.5 * (e0 + es)
-            bp, bm = 0.5 * (e0 + ee), 0.5 * (e0 + ew)
-            asum, bsum = ap + am, bp + bm
-            du = 4.0 * asum + bsum + drag
-            dv = asum + 4.0 * bsum + drag
-            n2, n4, s2, s4 = 0.5 * en, 0.25 * en, 0.5 * es, 0.25 * es
-            e2, e4, w2, w4 = 0.5 * ee, 0.25 * ee, 0.5 * ew, 0.25 * ew
-            vals = (
-                du, 4.0 * ap, 4.0 * am, bp, bm, n2 + e4, n2 + w4, s2 + e4, s2 + w4,
-                free / (du + 1.0 - free),
-                dv, ap, am, 4.0 * bp, 4.0 * bm, n4 + e2, n4 + w2, s4 + e2, s4 + w2,
-                free / (dv + 1.0 - free),
-            )
-            for k, v in enumerate(vals):
-                KF[m, k, at(r)] = v
-
-    def put(buf, t, c, r, d):
-        buf[t, c, 0, at(r, 8)] = d
-        buf[t, c, 1, at(r, 8)] = roll(d, -1)
-        buf[t, c, 2, at(r, 8)] = roll(d, 1)
-
-    def begin(t, r, iv, b):
-        for c in range(2):
-            d = iv[c] * b[c] * first_scale
-            R[t, c, at(r)] = b[c]
-            X[t, c, at(r)] = d
-            put(D0, t, c, r, d)
+        coefs(1, r)
 
     def sweep(k, lo, hi):
         src, dst = (D0, D1) if k % 2 == 0 else (D1, D0)
@@ -307,13 +332,10 @@
 
     @pl.loop(0, tiles, unroll=True)
     def _(r):
-        iv = [[KF[m, 9, at(r)], KF[m, 19, at(r)]] for m in range(2)]
-        free = K[2, at(r)]
-        for t in range(EP):
-            begin(t, r, iv[0], [free * F[t, c, at(r)] for c in range(2)])
+        iv = [KF[1, 9, at(r)], KF[1, 19, at(r)]]
         u, v = spread(*strips(0, r, pack(lambda t, c: F[t, c, at(r)])))
         fr = FRV[at(r)]
-        begin(EP, r, iv[1], [fr * u, fr * v])
+        begin(EP, r, iv, [fr * u, fr * v])
 
     for k in range(SWEEPS):
         sweep(k, 0, tiles)
@@ -348,8 +370,11 @@
             begin(t, r, iv[0], [free * (vel[t][c] - O[t, c, at(r)]) for c in range(2)])
         begin(EP, r, iv[1], [fr * (sv[c] - obs[c]) for c in range(2)])
 
-    out_copy = pltpu.make_async_copy(VO.at[:, :, pl.ds(HALO, rows)], vel_out, osem.at[0])
-    out_copy.start()
+    @pl.loop(0, own_tiles, unroll=True)
+    def _(r):
+        for t in range(EP):
+            for c in range(2):
+                vel_out[t, c, at(r)] = VO[t, c, at(r, 8)]
 
     for k in range(SWEEPS):
         sweep(k, 0 if k < SWEEPS - 1 else 1, tiles)
@@ -372,15 +397,11 @@
     @pl.loop(0, own_tiles, unroll=True)
     def _(r):
         q = PD[at(r, 8)] + PD[at(r, 9)]
-        GO[at(r)] = jnp.where(IM[at(r)] == 2, -0.25 * q, 0.0)
-
-    grad_copy = pltpu.make_async_copy(GO, grad_out, osem.at[1])
-    grad_copy.start()
+        grad_out[at(r)] = jnp.where(IM[at(r)] == 2, -0.25 * q, 0.0)
+
     for d in range(8):
         sent(d, 0)
         sent(d, 1)
-    out_copy.wait()
-    grad_copy.wait()
 
 
 def body(forcing, observed, viscosity, friction, ice_mask, dirichlet):
@@ -392,11 +413,11 @@
     velocity, gradient = pl.pallas_call(
         lambda *refs: kernel(rows, *refs),
         out_shape=(
-            jax.ShapeDtypeStruct(forcing.shape, f32),
-            jax.ShapeDtypeStruct(grid, f32),
+            pltpu.VMEM(forcing.shape, f32),
+            pltpu.VMEM(grid, f32),
         ),
         in_specs=[pl.BlockSpec(memory_space=pltpu.HBM)] * 6,
-        out_specs=(pl.BlockSpec(memory_space=pltpu.HBM),) * 2,
+        out_specs=(pl.BlockSpec(memory_space=pltpu.VMEM),) * 2,
         scratch_shapes=[
             V((EP, 2, ext, LANES), f32),
             V((EP, 2, ext, LANES), f32),
@@ -415,17 +436,15 @@
             V((EP, 2, ext, LANES), f32),
             V((ext, LANES), f32),
             V((8, LANES), f32),
-            V(grid, f32),
             pltpu.SemaphoreType.DMA((6,)),
-            pltpu.SemaphoreType.DMA((2,)),
             pltpu.SemaphoreType.DMA((8, 3)),
             pltpu.SemaphoreType.DMA((8, 3)),
         ],
         compiler_params=pltpu.CompilerParams(
-            collective_id=0, has_side_effects=True, vmem_limit_bytes=63 * 1024 * 1024
+            collective_id=0, has_side_effects=True, vmem_limit_bytes=24576 * 1024
         ),
         cost_estimate=pl.CostEstimate(flops=40_000_000, bytes_accessed=1_000_000, transcendentals=0),
-    )(forcing, observed, viscosity, friction, ice_mask, dirichlet)
+    )(*(pltpu.with_memory_space_constraint(a, pltpu.HBM) for a in (forcing, observed, viscosity, friction, ice_mask, dirichlet)))
     return velocity, gradient
 
 

time: 19.9 us -> 19.6 us (0.985)
  local copies, waits for them, and re-layouts: 2.3 us -> 1.32 us
  Pallas kernels: 16.8 us -> 17.5 us
    unnamed x4 -> x2, local copies, waits for them, and re-layouts: 2.3 us -> 1.32 us
    pallas_call x1, Pallas kernels: 16.8 us -> 17.5 us  [body(): pl.pallas_call(lambda *refs: kernel(rows, *refs), out_shape=(pltpu.VMEM(f...]
where the time goes in v3:
time: 19.6 us; the launch traced here: 19.5 us
  Pallas kernels  17.5 us (89%)
  local copies, waits for them, and re-layouts  1.32 us (7%)
  between operations  0.64 us (3%)
    pallas_call x1, Pallas kernels, body(): pl.pallas_call(lambda *refs: kernel(rows, *refs), out_shape=(pltpu.VMEM(f...  17.5 us
    unnamed x2, local copies, waits for them, and re-layouts  1.32 us

profile of v3, /device:TPU:0, one launch (start us, length us, event | category | flops | bytes accessed | tf_op | source)
XLA Modules:
  0.0 19.5 jit_solution(6629302203660358732)
XLA Ops:
  0.6 17.5 %shard_map.77 = (f32[4,2,64,128]{3,2,1,0:T(8,128)S(1)}, f32[64,128]{1,0:T(8,128)S(1)}) custom-call(f32[4,2,64,128]{3,2,1,0:T(8,128)} %refs_0_.1, f32[4,2,64,128]{3,2,1,0:T(8,128)} %refs_1_.1, f32[64,128]{1,0:T(8,128)} %refs_2_.1, f32[64,128]{1,0:T(8,128)} %refs_3_.1, s32[64,128]{1,0:T(8,128)} %refs_4_.1, s32[64,128]{1,0:T(8,128)} %refs_5_.1), custom_call_target="tpu_custom_call" | custom-call | flops 40000000 | bytes 1000000 | tf_op jit(solution)/shard_map/pallas_call | solution.py:413
  18.2 0.7 %copy.10 = f32[4,2,64,128]{3,2,1,0:T(8,128)} copy(f32[4,2,64,128]{3,2,1,0:T(8,128)S(1)} %get-tuple-element.2) | data formatting | bytes 524288
  18.9 0.6 %copy.11 = f32[64,128]{1,0:T(8,128)} copy(f32[64,128]{1,0:T(8,128)S(1)} %get-tuple-element.3) | data formatting | bytes 65536
